TPU v7x, 256 devices: a whole 4x4x8 slice. The times are simulated.
256 devices in a mesh: feat: 128 (over z, y, x), dp: 2 (over core).
Axes of the slice: x: 4, y: 4, z: 8, core: 2. Of those that a mesh axis runs over, the one named last changes fastest.
Arguments:
- grad_emb: bfloat16 [4096, 128, 128], P(('dp', 'feat')), may hold values from -0.59765625 to 0.59765625
- ids: int32 [4096, 128], P('dp', 'feat'), may hold values from 0 to 32767
- seeds: int32 [2, 1024], replicated, may hold values from 1 to 65520
- w_in: bfloat16 [128, 1024, 1024], P('feat'), may hold values from -0.1875 to 0.1875
- w_out: bfloat16 [128, 1024, 128], P('feat'), may hold values from -0.1875 to 0.1875
Outputs:
- grad_w_in: float32 [128, 1024, 1024], P('feat', None, 'dp')
- grad_w_out: float32 [128, 1024, 128], P('feat', 'dp')
All inputs are finite; a program needn't handle non-finite values.
Results may differ from a plain program's by a relative error of at most 0.004.
Values may be sent and summed in bfloat16 or wider, within the bound.
A program may use at most 64 MiB of HBM per device.

v0:
```python
import jax
import jax.numpy as jnp
from jax import lax
from jax.sharding import PartitionSpec as P

prime_mod = 65521


def encode(id_col, seeds):
    hashed = jnp.remainder(id_col[:, None] * seeds[0][None, :] + seeds[1][None, :], prime_mod)
    return (hashed.astype(jnp.float32) * (2.0 / (prime_mod - 1)) - 1.0).astype(jnp.bfloat16)


def mish(value):
    return value * jnp.tanh(jax.nn.softplus(value))


def mish_slope(value):
    squash = jnp.tanh(jax.nn.softplus(value))
    return squash + value * (1.0 - squash * squash) * jax.nn.sigmoid(value)


def contract_rows(left, right):
    return lax.dot_general(
        left, right, (((0,), (0,)), ((), ())), preferred_element_type=jnp.float32
    )


def on_device(grad_emb, ids, seeds, w_in, w_out):
    received = lax.all_to_all(grad_emb, "feat", split_axis=1, concat_axis=0, tiled=True)
    replicas = lax.axis_size("dp")
    upper = received[:, 0, :]
    encoding = encode(ids[:, 0], seeds)
    pre = jnp.dot(encoding, w_in[0], preferred_element_type=jnp.float32)
    hidden = mish(pre).astype(jnp.bfloat16)
    back_hidden = lax.dot_general(
        upper, w_out[0], (((1,), (1,)), ((), ())), preferred_element_type=jnp.float32
    )
    back_pre = (back_hidden * mish_slope(pre)).astype(jnp.bfloat16)

    def last_term(start, count, hidden=hidden, upper=upper):
        return contract_rows(hidden, upper)

    lasts = [
        lax.psum_scatter(
            last_term(jnp.int32(0), hidden.shape[1] // replicas * lax.axis_size("dp")),
            "dp",
            scatter_dimension=0,
            tiled=True,
        )
    ]
    firsts = [
        lax.psum_scatter(contract_rows(encoding, back_pre), "dp", scatter_dimension=1, tiled=True)
    ]
    return (jnp.stack(firsts), jnp.stack(lasts))


def solution(mesh):
    return jax.shard_map(
        on_device,
        mesh=mesh,
        in_specs=(
            P(("dp", "feat"), None, None),
            P("dp", "feat"),
            P(),
            P("feat", None, None),
            P("feat", None, None),
        ),
        out_specs=(P("feat", None, "dp"), P("feat", "dp", None)),
        check_vma=False,
    )
```

profile of v0, /device:TPU:1, one launch (start us, length us, event | category | flops | bytes accessed | tf_op | source)
XLA Modules:
  0.0 94.6 jit_solution(1734475163438413368)
XLA Ops:
  7.2 0.0 copy-start
  7.2 2.3 %copy.7 = bf16[16,128,128]{2,0,1:T(8,128)(2,1)} copy(bf16[16,128,128]{2,1,0:T(8,128)(2,1)} %param.5) | data formatting | bytes 1048576 | tf_op args[0]
  9.5 16.3 %all-to-all-start = ((bf16[16,128,128]{2,0,1:T(8,128)(2,1)}), bf16[16,128,128]{2,0,1:T(8,128)(2,1)S(1)}, u32[]{:S(2)}, u32[]{:S(2)}) async-start(bf16[16,128,128]{2,0,1:T(8,128)(2,1)} %copy.7), calls=%async_computation | async-start | bytes 1048576 | tf_op jit(solution)/shard_map/all_to_all | solution.py:30
  25.8 0.0 reduce-scatter.5.cloned.1.call-start
  25.9 0.8 fusion.27
  26.7 0.0 copy-done
  26.7 11.5 %fusion.10 = f32[2048,1024]{1,0:T(8,128)} fusion(s32[1024]{0:T(1024)S(1)} %bitcast.23, s32[1024]{0:T(1024)S(1)} %bitcast.21, s32[2048]{0:T(1024)} %bitcast.27, bf16[1,1024,1024]{2,1,0:T(8,128)(2,1)S(1)} %copy-done), kind=kOutput, calls=%fused_computation.15 | convolution fusion | flops 4320133120 | bytes 10502144 | tf_op jit(solution)/shard_map/dot_general | solution.py:34
  38.2 5.9 %all-to-all-done = bf16[16,128,128]{2,0,1:T(8,128)(2,1)S(1)} async-done(((bf16[16,128,128]{2,0,1:T(8,128)(2,1)}), bf16[16,128,128]{2,0,1:T(8,128)(2,1)S(1)}, u32[]{:S(2)}, u32[]{:S(2)}) %all-to-all-start) | async-done | bytes 524320 | tf_op jit(solution)/shard_map/all_to_all | solution.py:30
  44.1 0.0 copy-start.1
  44.1 0.0 copy-start.2
  44.1 8.5 %fusion.12 = f32[1024,128]{1,0:T(8,128)} fusion(bf16[2048,128]{1,0:T(8,128)(2,1)S(1)} %bitcast.19, f32[2048,1024]{1,0:T(8,128)} %fusion.10), kind=kOutput, calls=%fused_computation.16 | convolution fusion | flops 553648128 | bytes 9437184 | tf_op jit(solution)/shard_map/dot_general | solution.py:24
  52.6 0.0 reduce-scatter.5.cloned.1.call-update
  52.7 0.2 reduce-scatter.3.cloned.1.call-start
  52.9 0.0 copy-done.1
  52.9 0.0 copy-done.2
  52.9 21.4 %fusion.8 = f32[1024,1024]{1,0:T(8,128)} fusion(s32[1024]{0:T(1024)S(1)} %bitcast.24, s32[1024]{0:T(1024)S(1)} %bitcast.22, s32[2048]{0:T(1024)S(1)} %bitcast.28, f32[2048,1024]{1,0:T(8,128)} %fusion.10, bf16[2048,128]{1,0:T(8,128)(2,1)S(1)} %bitcast.20, bf16[1,1024,128]{2,1,0:T(8,128)(2,1)S(1)} %copy-done.1), kind=kOutput, calls=%fused_computation.14 | convolution fusion | flops 4890558464 | bytes 13385728 | tf_op jit(solution)/shard_map/dot_general | solution.py:24
  74.3 0.0 reduce-scatter.3.cloned.1.call-update
  74.3 0.0 reduce-scatter.5.cloned.1.call-done
  74.3 13.4 %reduce-scatter.3.cloned.1.call-done = f32[1024,512]{1,0:T(8,128)} async-done(((f32[1024,1024]{1,0:T(8,128)}), f32[1024,512]{1,0:T(8,128)}) %reduce-scatter.3.cloned.1.call-update) | async-done | bytes 2097168 | tf_op jit(solution)/shard_map/reduce_scatter | solution.py:53
Async XLA Ops:
  7.2 19.5 %copy-start = (bf16[1,1024,1024]{2,1,0:T(8,128)(2,1)S(1)}, bf16[1,1024,1024]{2,1,0:T(8,128)(2,1)}, u32[]{:S(2)}) copy-start(bf16[1,1024,1024]{2,1,0:T(8,128)(2,1)} %param.8) | copy-start | bytes 6291460
  9.5 34.6 %all-to-all-start = ((bf16[16,128,128]{2,0,1:T(8,128)(2,1)}), bf16[16,128,128]{2,0,1:T(8,128)(2,1)S(1)}, u32[]{:S(2)}, u32[]{:S(2)}) async-start(bf16[16,128,128]{2,0,1:T(8,128)(2,1)} %copy.7), calls=%async_computation | async-start | bytes 1048576 | tf_op jit(solution)/shard_map/all_to_all | solution.py:30
  25.8 48.5 %reduce-scatter.5.cloned.1.call-start = ((), (), s32[]{:S(2)}) async-start(), calls=%async_computation.4 | async-start | bytes 786432 | tf_op jit(solution)/shard_map/reduce_scatter | solution.py:45
  44.1 8.7 %copy-start.1 = (bf16[1,1024,128]{2,1,0:T(8,128)(2,1)S(1)}, bf16[1,1024,128]{2,1,0:T(8,128)(2,1)}, u32[]{:S(2)}) copy-start(bf16[1,1024,128]{2,1,0:T(8,128)(2,1)} %param.9) | copy-start | bytes 786436
  44.1 8.8 %copy-start.2 = (s32[2048,1]{0,1:T(1,128)S(1)}, s32[2048,1]{0,1:T(1,128)}, u32[]{:S(2)}) copy-start(s32[2048,1]{0,1:T(1,128)} %param.6) | copy-start | bytes 24580
  52.7 35.1 %reduce-scatter.3.cloned.1.call-start = ((), (), s32[]{:S(2)}) async-start(), calls=%async_computation.3 | async-start | bytes 6291456 | tf_op jit(solution)/shard_map/reduce_scatter | solution.py:53
Sparse Core Ops, SparseCore 0:
  52.8 9.3 reduce-scatter.4
  74.4 13.2 reduce-scatter.2
where the time goes:
time: 94.9 us; the launch traced here: 94.6 us
  matrix products  41.4 us (44%)
  waiting for transfers between devices  19.3 us (20%)
  starting transfers between devices  16.6 us (17%)
  between operations  14.1 us (15%)
  local copies, waits for them, and re-layouts  3.12 us (3%)
    dot_general x2, matrix products, contract_rows(): lax.dot_general(left, right, (((0,), (0,)), ((), ())), preferred_element_...  29.9 us
    all_to_all x1, starting transfers between devices, on_device(): lax.all_to_all(grad_emb, 'feat', split_axis=1, concat_axis=0, tiled=True)  16.3 us
    reduce_scatter x1, waiting for transfers between devices, on_device(): lax.psum_scatter(contract_rows(encoding, back_pre), 'dp', scatter_dimensi...  13.4 us
    dot_general x1, matrix products, on_device(): pre = jnp.dot(encoding, w_in[0], preferred_element_type=jnp.float32)  11.5 us
    all_to_all x1, waiting for transfers between devices, on_device(): lax.all_to_all(grad_emb, 'feat', split_axis=1, concat_axis=0, tiled=True)  5.9 us
    unnamed x7, local copies, waits for them, and re-layouts  2.34 us
  transfers between devices with their start and end apart: 3, of which 2 were waited for; matrix products, arithmetic and copies ran while one was open for 36% of the time, Pallas kernels for 0%

commit v1 on v0

v1 whole, which is shorter than its diff:
```python
import functools

import jax
import jax.numpy as jnp
from jax import lax
from jax.experimental import pallas as pl
from jax.experimental.pallas import tpu as pltpu
from jax.sharding import PartitionSpec as P

PRIME = 65521
HALF = 32760
MESH = pl.DeviceIdType.MESH
NX, NY, NZ = 4, 4, 8
FEATS = 128
ROWS = 16
K = 1024
H2 = 512
E = 128
HC = 512
F32 = jnp.float32
BF16 = jnp.bfloat16


def place():
    me = lax.axis_index("feat")
    return me, me // (NX * NY), (me // NX) % NY, me % NX


def target(step):
    _, mz, my, mx = place()
    plane, hop = step // NZ, step % NZ
    dz = jnp.where(hop % 2 == 1, (hop + 1) // 2, (NZ - hop // 2) % NZ)
    dy, dx = plane // NX, plane % NX
    z, y, x = (mz + dz) % NZ, (my + dy) % NY, (mx + dx) % NX
    return z * (NX * NY) + y * NX + x, dy


def fold(x):
    r = (x >> 16) * 15 + (x & 65535)
    return jnp.where(r >= PRIME, r - PRIME, r)


def coefficient_rows(seeds):
    a, b = seeds[0:1, :], seeds[1:2, :]
    a1, a2 = fold(a * 32), fold(a * 1024)
    shift = fold(b + 16 * (a + a1 + a2) + (PRIME - HALF))
    rows = []
    for c in (a, a1, a2, shift):
        c = jnp.where(c > HALF, c - PRIME, c)
        high = (c + 128) >> 8
        rows += [high * 256, c - high * 256]
    rows.append(jnp.zeros((128 - len(rows), K), jnp.int32))
    return jnp.concatenate(rows, axis=0).astype(F32)


def digits(ids, out, base):
    lane = lax.broadcasted_iota(jnp.int32, (1, 128), 1)
    row = lax.broadcasted_iota(jnp.int32, (16, 128), 0)
    turned = pltpu.roll(ids, 64, 1)
    for y in range(NY):
        for m in range(NZ // 2):
            r0 = 4 * m + y // 2
            r1 = r0 + 2
            first, second = (ids, turned) if y % 2 == 0 else (turned, ids)
            line = jnp.where(lane < 64, first[r0 : r0 + 1, :], second[r1 : r1 + 1, :])
            wide = jnp.broadcast_to(line, (16, 128))
            digit = ((wide >> ((row >> 1) * 5)) & 31) - 16
            digit = jnp.where(row < 6, digit, jnp.where(row < 8, 1, 0))
            out[2 * y + base, :, m * 128 : (m + 1) * 128] = digit.astype(F32).astype(BF16)


def nt(left, right):
    return lax.dot_general(left, right, (((1,), (1,)), ((), ())), preferred_element_type=F32)


def kernel(
    g_hbm, ids_hbm, seeds_hbm, win_hbm, wout_hbm, gin_hbm, gout_hbm,
    g_v, g_f, send, upper, ids_v, seeds_v, win_v, winT, wout_v, coef, digit, enc, pre, hid, slope, acc, acc_o,
    load, out_sem, send_sem, recv_sem, ids_send, ids_recv, pass_send, pass_recv,
):
    me, mz, my, mx = place()
    core = lax.axis_index("dp")
    sibling = {"dp": 1 - core}
    loads = [
        pltpu.make_async_copy(g_hbm, g_v, load.at[0]),
        pltpu.make_async_copy(ids_hbm, ids_v.at[0], load.at[1]),
        pltpu.make_async_copy(seeds_hbm, seeds_v, load.at[2]),
        pltpu.make_async_copy(win_hbm.at[0, :, pl.ds(pl.multiple_of(core * H2, H2), H2)], win_v, load.at[3]),
        pltpu.make_async_copy(wout_hbm.at[0, pl.ds(pl.multiple_of(core * H2, H2), H2), :], wout_v, load.at[4]),
    ]
    for c in loads:
        c.start()

    barrier = pltpu.get_barrier_semaphore()

    @pl.loop(1, FEATS)
    def _(i):
        pl.semaphore_signal(barrier, inc=1, device_id={"feat": (me + i) % FEATS}, device_id_type=MESH)

    pl.semaphore_signal(barrier, inc=1, device_id=sibling, device_id_type=MESH)

    loads[0].wait()
    g_f[...] = g_v[...].astype(F32).reshape(ROWS * FEATS, E)

    @pl.loop(0, FEATS, unroll=8)
    def _(f):
        send[f] = g_f[pl.ds(f, ROWS, stride=FEATS), :].astype(BF16)

    slot = my * (NZ * NX) + mz * NX + mx
    upper[0, slot] = send[me]
    loads[1].wait()
    pl.semaphore_wait(barrier, FEATS)

    ids_copy = pltpu.make_async_remote_copy(
        src_ref=ids_v.at[0], dst_ref=ids_v.at[1], send_sem=ids_send, recv_sem=ids_recv,
        device_id=sibling, device_id_type=MESH,
    )
    ids_copy.start()

    @pl.loop(1, FEATS)
    def _(i):
        to, dy = target(i)
        pltpu.make_async_remote_copy(
            src_ref=send.at[to], dst_ref=upper.at[0, slot], send_sem=send_sem, recv_sem=recv_sem.at[dy],
            device_id={"feat": to}, device_id_type=MESH,
        ).start()

    loads[2].wait()
    coef[...] = jnp.transpose(coefficient_rows(seeds_v[...]))[:, :16].astype(BF16)
    loads[3].wait()
    for b in range(K // 128):
        winT[:, b * 128 : (b + 1) * 128] = jnp.transpose(win_v[b * 128 : (b + 1) * 128, :].astype(F32)).astype(BF16)
    digits(ids_v[0], digit, 0)
    ids_copy.wait()
    digits(ids_v[1], digit, 1)

    @pl.loop(0, 8)
    def _(i):
        for r in range(0, K, 256):
            w = jnp.dot(coef[r : r + 256, :], digit[i], preferred_element_type=F32)
            turns = jnp.round(w * F32(1.0 / PRIME))
            enc[i, r : r + 256, :] = ((w - turns * F32(PRIME)) * F32(2.0 / (PRIME - 1))).astype(BF16)
        pre[...] = jnp.dot(winT[...], enc[i], preferred_element_type=F32)
        for r in range(0, H2, 32):
            v = pre[r : r + 32, :]
            e = jnp.exp(jnp.minimum(v, 20.0))
            square = e * e
            half = 0.5 * square + e
            both = square + e
            inv = 1.0 / (half + 1.0)
            u = v * inv
            hid[i, r : r + 32, :] = (half * u).astype(BF16)
            slope[i, r : r + 32, :] = (half + both * u) * inv

    loads[4].wait()
    acc[...] = jnp.zeros_like(acc)
    acc_o[...] = jnp.zeros_like(acc_o)

    def part(y, side):
        i = 2 * y + side
        up = upper[side, pl.ds(y * (NZ * NX), NZ * NX)].reshape(HC, E)
        back = nt(wout_v[...], up)
        back_pre = (back * slope[i]).astype(BF16)
        acc_o[...] += jnp.dot(hid[i], up, preferred_element_type=F32)
        acc[...] += nt(enc[i], back_pre)

    def received(dy, y, count):
        first = y * (NZ * NX)
        return pltpu.make_async_remote_copy(
            src_ref=send.at[pl.ds(0, count)], dst_ref=upper.at[0, pl.ds(first, count)], send_sem=send_sem,
            recv_sem=recv_sem.at[dy], device_id=sibling, device_id_type=MESH,
        )

    def passed(dy, y):
        first = y * (NZ * NX)
        return pltpu.make_async_remote_copy(
            src_ref=upper.at[0, pl.ds(first, NZ * NX)], dst_ref=upper.at[1, pl.ds(first, NZ * NX)],
            send_sem=pass_send.at[dy], recv_sem=pass_recv.at[dy], device_id=sibling, device_id_type=MESH,
        )

    @pl.loop(0, NY)
    def _(dy):
        y = (my - dy + NY) % NY

        @pl.when(dy == 0)
        def _():
            received(dy, y, NZ * NX - 1).wait_recv()

        @pl.when(dy > 0)
        def _():
            received(dy, y, NZ * NX).wait_recv()

        onward = passed(dy, y)
        onward.start()
        part(y, 0)
        onward.wait()
        part(y, 1)

    outs = [
        pltpu.make_async_copy(acc, gin_hbm.at[0], out_sem.at[0]),
        pltpu.make_async_copy(acc_o, gout_hbm.at[0], out_sem.at[1]),
    ]
    for c in outs:
        c.start()
    pltpu.make_async_remote_copy(
        src_ref=send.at[pl.ds(0, FEATS - 1)], dst_ref=upper.at[0, pl.ds(0, FEATS - 1)], send_sem=send_sem,
        recv_sem=recv_sem.at[0], device_id=sibling, device_id_type=MESH,
    ).wait_send()
    for c in outs:
        c.wait()


def on_device(grad_emb, ids, seeds, w_in, w_out):
    dma = pltpu.SemaphoreType.DMA
    gin, gout = pl.pallas_call(
        kernel,
        out_shape=(jax.ShapeDtypeStruct((1, K, H2), F32), jax.ShapeDtypeStruct((1, H2, E), F32)),
        in_specs=[pl.BlockSpec(memory_space=pl.ANY)] * 5,
        out_specs=[pl.BlockSpec(memory_space=pl.ANY)] * 2,
        scratch_shapes=[
            pltpu.VMEM((ROWS, FEATS, E), BF16),
            pltpu.VMEM((ROWS * FEATS, E), F32),
            pltpu.VMEM((FEATS, ROWS, E), BF16),
            pltpu.VMEM((2, FEATS, ROWS, E), BF16),
            pltpu.VMEM((2, 16, 128), jnp.int32),
            pltpu.VMEM((2, K), jnp.int32),
            pltpu.VMEM((K, H2), BF16),
            pltpu.VMEM((H2, K), BF16),
            pltpu.VMEM((H2, E), BF16),
            pltpu.VMEM((K, 16), BF16),
            pltpu.VMEM((8, 16, HC), BF16),
            pltpu.VMEM((8, K, HC), BF16),
            pltpu.VMEM((H2, HC), F32),
            pltpu.VMEM((8, H2, HC), BF16),
            pltpu.VMEM((8, H2, HC), F32),
            pltpu.VMEM((K, H2), F32),
            pltpu.VMEM((H2, E), F32),
            dma((5,)), dma((2,)), dma, dma((NY,)), dma, dma, dma((NY,)), dma((NY,)),
        ],
        compiler_params=pltpu.CompilerParams(
            collective_id=0, has_side_effects=True, vmem_limit_bytes=56 * 2**20
        ),
        name="feature_backward",
    )(grad_emb, ids.reshape(16, 128), seeds, w_in, w_out)
    return gin, gout


def solution(mesh):
    return jax.shard_map(
        on_device,
        mesh=mesh,
        in_specs=(
            P(("dp", "feat"), None, None),
            P("dp", "feat"),
            P(),
            P("feat", None, None),
            P("feat", None, None),
        ),
        out_specs=(P("feat", None, "dp"), P("feat", "dp", None)),
        check_vma=False,
    )
```

time: 94.9 us -> 45.9 us (0.48)
  matrix products: 41.4 us -> 0 us
  Pallas kernels: 0 us -> 41.3 us
  waiting for transfers between devices: 19.3 us -> 0 us
  starting transfers between devices: 16.6 us -> 0 us
  between operations: 14.1 us -> 0.65 us
    dot_general x3 -> x0, matrix products: 41.4 us -> none  [the longest x2 29.9 us: contract_rows(): lax.dot_general(left, right, (((0,), (0,)), ((), ())), preferred_element_...]
    pallas_call x0 -> x1, Pallas kernels: none -> 41.3 us  [on_device(): pl.pallas_call(kernel, out_shape=(jax.ShapeDtypeStruct((1, K, H2), F32),...]
    all_to_all x1 -> x0, starting transfers between devices: 16.3 us -> none  [on_device(): lax.all_to_all(grad_emb, 'feat', split_axis=1, concat_axis=0, tiled=True)]
    reduce_scatter x2 -> x0, waiting for transfers between devices: 13.4 us -> none  [the longest x1 13.4 us: on_device(): lax.psum_scatter(contract_rows(encoding, back_pre), 'dp', scatter_dimensi...]
    all_to_all x1 -> x0, waiting for transfers between devices: 5.9 us -> none  [on_device(): lax.all_to_all(grad_emb, 'feat', split_axis=1, concat_axis=0, tiled=True)]
    unnamed x7 -> x4, local copies, waits for them, and re-layouts: 2.34 us -> 3.83 us
  transfers between devices with their start and end apart: 3 -> 0, of which waited for: 2 -> 0; matrix products, arithmetic and copies ran while one was open for 36% -> 0% of each run, Pallas kernels for 0% -> 0%
where the time goes in v1:
time: 45.9 us; the launch traced here: 45.8 us
  Pallas kernels  41.3 us (90%)
  local copies, waits for them, and re-layouts  3.83 us (8%)
  between operations  0.65 us (1%)
    pallas_call x1, Pallas kernels, on_device(): pl.pallas_call(kernel, out_shape=(jax.ShapeDtypeStruct((1, K, H2), F32),...  41.3 us
    unnamed x4, local copies, waits for them, and re-layouts  3.83 us

profile of v1, /device:TPU:1, one launch (start us, length us, event | category | flops | bytes accessed | tf_op | source)
XLA Modules:
  0.0 45.8 jit_solution(11902295490654502846)
XLA Ops:
  0.6 41.3 %feature_backward.1 = (f32[1,1024,512]{2,1,0:T(8,128)}, f32[1,512,128]{2,1,0:T(8,128)}) custom-call(bf16[16,128,128]{2,1,0:T(8,128)(2,1)} %g_hbm.1, s32[16,128]{1,0:T(8,128)} %bitcast.1, s32[2,1024]{1,0:T(2,128)} %seeds_hbm.1, bf16[1,1024,1024]{2,1,0:T(8,128)(2,1)} %win_hbm.1, bf16[1,1024,128]{2,1,0:T(8,128)(2,1)} %wout_hbm.1), custom_call_target="tpu_custom_call" | custom-call | tf_op jit(solution)/shard_map/feature_backward/pallas_call | solution.py:215
  42.0 0.0 copy-start
  42.0 3.1 %copy.9 = f32[1,1024,512]{2,1,0:T(8,128)} copy(f32[1,1024,512]{2,1,0:T(8,128)} %get-tuple-element.4) | data formatting | bytes 4194304
  45.1 0.0 copy-done
  45.1 0.7 %copy.10 = f32[1,512,128]{2,1,0:T(8,128)} copy(f32[1,512,128]{2,1,0:T(8,128)S(1)} %copy-done) | data formatting | bytes 524288
Async XLA Ops:
  42.0 3.1 %copy-start = (f32[1,512,128]{2,1,0:T(8,128)S(1)}, f32[1,512,128]{2,1,0:T(8,128)}, u32[]{:S(2)}) copy-start(f32[1,512,128]{2,1,0:T(8,128)} %get-tuple-element.5) | copy-start | bytes 786436

commit v2 on v1

v2 whole, which is shorter than its diff:
```python
import functools

import jax
import jax.numpy as jnp
from jax import lax
from jax.experimental import pallas as pl
from jax.experimental.pallas import tpu as pltpu
from jax.sharding import PartitionSpec as P

PRIME = 65521
HALF = 32760
ONE = 2**21
MESH = pl.DeviceIdType.MESH
NX, NY, NZ = 4, 4, 8
FEATS = 128
ROWS = 16
K = 1024
H2 = 512
E = 128
HC = 512
F32 = jnp.float32
BF16 = jnp.bfloat16


def place():
    me = lax.axis_index("feat")
    return me, me // (NX * NY), (me // NX) % NY, me % NX


def wrap(value, size):
    return jnp.where(value >= size, value - size, value)


def fold(x):
    return (x >> 16) * 15 + (x & 65535)


def coefficient_rows(seeds):
    row = lax.broadcasted_iota(jnp.int32, (16, K), 0)
    shift = jnp.broadcast_to(seeds[1:2, :] + (PRIME - HALF), (16, K))
    x = fold(fold(jnp.where(row < 15, jnp.broadcast_to(seeds[0:1, :], (16, K)) << row, shift)))
    x = jnp.where(x >= PRIME, x - PRIME, x)
    x = jnp.where(x > HALF, x - PRIME, x)
    fixed = jnp.round(x.astype(F32) * F32(ONE / PRIME)).astype(jnp.int32)
    high = (fixed + 8192) >> 14
    rest = fixed - (high << 14)
    middle = (rest + 64) >> 7
    parts = [high << 14, middle << 7, rest - (middle << 7)]
    rows = [p.astype(F32) * F32(1.0 / ONE) for p in parts]
    return jnp.concatenate(rows + [jnp.zeros((128 - 48, K), F32)], axis=0)


def bits(ids, out, base):
    lane = lax.broadcasted_iota(jnp.int32, (1, 128), 1)
    row = lax.broadcasted_iota(jnp.int32, (16, 128), 0)
    turned = pltpu.roll(ids, 64, 1)
    for y in range(NY):
        for m in range(NZ // 2):
            r0 = 4 * m + y // 2
            r1 = r0 + 2
            first, second = (ids, turned) if y % 2 == 0 else (turned, ids)
            line = jnp.where(lane < 64, first[r0 : r0 + 1, :], second[r1 : r1 + 1, :])
            wide = jnp.broadcast_to(line, (16, 128))
            bit = jnp.where(row < 15, (wide >> row) & 1, 1).astype(F32).astype(BF16)
            for r in range(0, 48, 16):
                out[2 * y + base, r : r + 16, m * 128 : (m + 1) * 128] = bit


def nt(left, right):
    return lax.dot_general(left, right, (((1,), (1,)), ((), ())), preferred_element_type=F32)


def kernel(
    g_hbm, ids_hbm, seeds_hbm, win_hbm, wout_hbm, acc, acc_o,
    g_v, g_f, send, upper, ids_v, seeds_v, win_v, winT, wout_v, coef, digit, enc_a, enc_b, pre_a, pre_b, hid, slope,
    load, send_sem, recv_sem, ids_send, ids_recv, pass_send, pass_recv,
):
    me, mz, my, mx = place()
    core = lax.axis_index("dp")
    sibling = {"dp": 1 - core}
    loads = [
        pltpu.make_async_copy(g_hbm, g_v, load.at[0]),
        pltpu.make_async_copy(ids_hbm, ids_v.at[0], load.at[1]),
        pltpu.make_async_copy(seeds_hbm, seeds_v, load.at[2]),
        pltpu.make_async_copy(win_hbm.at[0, :, pl.ds(pl.multiple_of(core * H2, H2), H2)], win_v, load.at[3]),
        pltpu.make_async_copy(wout_hbm.at[0, pl.ds(pl.multiple_of(core * H2, H2), H2), :], wout_v, load.at[4]),
    ]
    for c in loads:
        c.start()

    barrier = pltpu.get_barrier_semaphore()

    @pl.loop(0, FEATS - 1, unroll=True)
    def _(i):
        other = jnp.where(i >= me, i + 1, i)
        pl.semaphore_signal(barrier, inc=1, device_id={"feat": other}, device_id_type=MESH)

    pl.semaphore_signal(barrier, inc=1, device_id=sibling, device_id_type=MESH)

    loads[0].wait()
    g_f[...] = g_v[...].astype(F32).reshape(ROWS * FEATS, E)

    @pl.loop(0, FEATS, unroll=8)
    def _(f):
        send[f] = g_f[pl.ds(f, ROWS, stride=FEATS), :].astype(BF16)

    slot = my * (NZ * NX) + mz * NX + mx
    upper[0, slot] = send[me]
    loads[1].wait()
    pl.semaphore_wait(barrier, FEATS)

    ids_copy = pltpu.make_async_remote_copy(
        src_ref=ids_v.at[0], dst_ref=ids_v.at[1], send_sem=ids_send, recv_sem=ids_recv,
        device_id=sibling, device_id_type=MESH,
    )
    ids_copy.start()

    columns = [wrap(mz + dz, NZ) * (NX * NY) for dz in (0, 1, 7, 2, 6, 3, 5, 4)]

    def send_to(to, dy):
        pltpu.make_async_remote_copy(
            src_ref=send.at[to], dst_ref=upper.at[0, slot], send_sem=send_sem, recv_sem=recv_sem.at[dy],
            device_id={"feat": to}, device_id_type=MESH,
        ).start()

    @pl.loop(0, NY)
    def _(dy):
        y = wrap(my + dy, NY) * NX

        @pl.loop(0, NX)
        def _(dx):
            near = y + wrap(mx + dx, NX)

            @pl.when(dy + dx > 0)
            def _():
                send_to(columns[0] + near, dy)

            for column in columns[1:]:
                send_to(column + near, dy)

    loads[2].wait()
    coef[...] = jnp.transpose(coefficient_rows(seeds_v[...]))[:, :48].astype(BF16)
    loads[3].wait()
    for b in range(K // 128):
        winT[:, b * 128 : (b + 1) * 128] = jnp.transpose(win_v[b * 128 : (b + 1) * 128, :].astype(F32)).astype(BF16)
    bits(ids_v[0], digit, 0)
    ids_copy.wait()
    bits(ids_v[1], digit, 1)

    def encode(out, j, i):
        for r in range(0, K, 256):
            w = jnp.dot(coef[r : r + 256, :], digit[i], preferred_element_type=F32)
            out[j, r : r + 256, :] = ((w - jnp.round(w)) * F32(2.0 * PRIME / (PRIME - 1))).astype(BF16)

    def forward(block, out):
        out[...] = jnp.dot(winT[...], block, preferred_element_type=F32)

    def activate(pre, i):
        for r in range(0, H2, 16):
            v = pre[r : r + 16, :]
            e = jnp.exp(jnp.minimum(v, 20.0))
            square = e * e
            half = 0.5 * square + e
            both = square + e
            inv = 1.0 / (half + 1.0)
            u = v * inv
            hid[i, r : r + 16, :] = (half * u).astype(BF16)
            slope[i, r : r + 16, :] = (half + both * u) * inv

    encode(enc_a, 0, 0)
    pre_b[...] = jnp.zeros_like(pre_b)

    @pl.loop(0, NY)
    def _(j):
        forward(enc_a[j], pre_a)
        encode(enc_b, j, 2 * j + 1)
        activate(pre_b, (2 * j + 7) % 8)
        forward(enc_b[j], pre_b)
        encode(enc_a, (j + 1) % NY, (2 * j + 2) % 8)
        activate(pre_a, 2 * j)

    activate(pre_b, 7)
    loads[4].wait()
    acc[...] = jnp.zeros_like(acc)
    acc_o[...] = jnp.zeros_like(acc_o)

    def part(y, side):
        i = 2 * y + side
        up = upper[side, pl.ds(y * (NZ * NX), NZ * NX)].reshape(HC, E)
        back = nt(wout_v[...], up)
        back_pre = (back * slope[i]).astype(BF16)
        acc_o[0] += jnp.dot(hid[i], up, preferred_element_type=F32)
        acc[0] += nt((enc_a, enc_b)[side][y], back_pre)

    def received(dy, y, count):
        first = y * (NZ * NX)
        return pltpu.make_async_remote_copy(
            src_ref=send.at[pl.ds(0, count)], dst_ref=upper.at[0, pl.ds(first, count)], send_sem=send_sem,
            recv_sem=recv_sem.at[dy], device_id=sibling, device_id_type=MESH,
        )

    def passed(dy, y):
        first = y * (NZ * NX)
        return pltpu.make_async_remote_copy(
            src_ref=upper.at[0, pl.ds(first, NZ * NX)], dst_ref=upper.at[1, pl.ds(first, NZ * NX)],
            send_sem=pass_send.at[dy], recv_sem=pass_recv.at[dy], device_id=sibling, device_id_type=MESH,
        )

    @pl.loop(0, NY)
    def _(dy):
        y = (my - dy + NY) % NY

        @pl.when(dy == 0)
        def _():
            received(dy, y, NZ * NX - 1).wait_recv()

        @pl.when(dy > 0)
        def _():
            received(dy, y, NZ * NX).wait_recv()

        onward = passed(dy, y)
        onward.start()
        part(y, 0)
        onward.wait()
        part(y, 1)

    pltpu.make_async_remote_copy(
        src_ref=send.at[pl.ds(0, FEATS - 1)], dst_ref=upper.at[0, pl.ds(0, FEATS - 1)], send_sem=send_sem,
        recv_sem=recv_sem.at[0], device_id=sibling, device_id_type=MESH,
    ).wait_send()


def write_out(acc, acc_o, gin_hbm, gout_hbm, sem):
    copies = [
        pltpu.make_async_copy(acc, gin_hbm, sem.at[0]),
        pltpu.make_async_copy(acc_o, gout_hbm, sem.at[1]),
    ]
    for c in copies:
        c.start()
    for c in copies:
        c.wait()


def on_device(grad_emb, ids, seeds, w_in, w_out):
    dma = pltpu.SemaphoreType.DMA
    sums = pl.pallas_call(
        kernel,
        out_shape=(pltpu.VMEM((1, K, H2), F32), pltpu.VMEM((1, H2, E), F32)),
        in_specs=[pl.BlockSpec(memory_space=pl.ANY)] * 5,
        out_specs=[pl.BlockSpec(memory_space=pltpu.VMEM)] * 2,
        scratch_shapes=[
            pltpu.VMEM((ROWS, FEATS, E), BF16),
            pltpu.VMEM((ROWS * FEATS, E), F32),
            pltpu.VMEM((FEATS, ROWS, E), BF16),
            pltpu.VMEM((2, FEATS, ROWS, E), BF16),
            pltpu.VMEM((2, 16, 128), jnp.int32),
            pltpu.VMEM((2, K), jnp.int32),
            pltpu.VMEM((K, H2), BF16),
            pltpu.VMEM((H2, K), BF16),
            pltpu.VMEM((H2, E), BF16),
            pltpu.VMEM((K, 48), BF16),
            pltpu.VMEM((8, 48, HC), BF16),
            pltpu.VMEM((NY, K, HC), BF16),
            pltpu.VMEM((NY, K, HC), BF16),
            pltpu.VMEM((H2, HC), F32),
            pltpu.VMEM((H2, HC), F32),
            pltpu.VMEM((8, H2, HC), BF16),
            pltpu.VMEM((8, H2, HC), F32),
            dma((5,)), dma, dma((NY,)), dma, dma, dma((NY,)), dma((NY,)),
        ],
        compiler_params=pltpu.CompilerParams(
            collective_id=0, has_side_effects=True, vmem_limit_bytes=48 * 2**20
        ),
        name="feature_backward",
    )(*[
        pltpu.with_memory_space_constraint(x, pltpu.HBM)
        for x in (grad_emb, ids.reshape(16, 128), seeds, w_in, w_out)
    ])
    return pl.pallas_call(
        write_out,
        out_shape=(pltpu.HBM((1, K, H2), F32), pltpu.HBM((1, H2, E), F32)),
        in_specs=[pl.BlockSpec(memory_space=pltpu.VMEM)] * 2,
        out_specs=[pl.BlockSpec(memory_space=pltpu.HBM)] * 2,
        scratch_shapes=[dma((2,))],
        name="write_out",
    )(*[pltpu.with_memory_space_constraint(x, pltpu.VMEM) for x in sums])


def solution(mesh):
    return jax.shard_map(
        on_device,
        mesh=mesh,
        in_specs=(
            P(("dp", "feat"), None, None),
            P("dp", "feat"),
            P(),
            P("feat", None, None),
            P("feat", None, None),
        ),
        out_specs=(P("feat", None, "dp"), P("feat", "dp", None)),
        check_vma=False,
    )
```

time: 45.9 us -> 36.5 us (0.80)
  Pallas kernels: 41.3 us -> 35.7 us
  local copies, waits for them, and re-layouts: 3.83 us -> 0 us
    pallas_call x1 -> x2, Pallas kernels: 41.3 us -> 35.7 us  [the longest x1 34.3 us: on_device(): pl.pallas_call(kernel, out_shape=(pltpu.VMEM((1, K, H2), F32), pltpu.VMEM...]
    unnamed x4 -> x0, local copies, waits for them, and re-layouts: 3.83 us -> none
where the time goes in v2:
time: 36.5 us; the launch traced here: 36.4 us
  Pallas kernels  35.7 us (98%)
  between operations  0.64 us (2%)
    pallas_call x1, Pallas kernels, on_device(): pl.pallas_call(kernel, out_shape=(pltpu.VMEM((1, K, H2), F32), pltpu.VMEM...  34.3 us
    pallas_call x1, Pallas kernels, on_device(): pl.pallas_call(write_out, out_shape=(pltpu.HBM((1, K, H2), F32), pltpu.HB...  1.41 us

profile of v2, /device:TPU:1, one launch (start us, length us, event | category | flops | bytes accessed | tf_op | source)
XLA Modules:
  0.0 36.4 jit_solution(17421528740994689264)
XLA Ops:
  0.6 34.3 %feature_backward.1 = (f32[1,1024,512]{2,1,0:T(8,128)S(1)}, f32[1,512,128]{2,1,0:T(8,128)S(1)}) custom-call(bf16[16,128,128]{2,1,0:T(8,128)(2,1)} %g_hbm.1, s32[16,128]{1,0:T(8,128)} %bitcast.1, s32[2,1024]{1,0:T(2,128)} %seeds_hbm.1, bf16[1,1024,1024]{2,1,0:T(8,128)(2,1)} %win_hbm.1, bf16[1,1024,128]{2,1,0:T(8,128)(2,1)} %wout_hbm.1), custom_call_target="tpu_custom_call" | custom-call | tf_op jit(solution)/shard_map/feature_backward/pallas_call | solution.py:246
  35.0 1.4 %write_out.1 = (f32[1,1024,512]{2,1,0:T(8,128)}, f32[1,512,128]{2,1,0:T(8,128)}) custom-call(f32[1,1024,512]{2,1,0:T(8,128)S(1)} %get-tuple-element.4.acc, f32[1,512,128]{2,1,0:T(8,128)S(1)} %get-tuple-element.5.acc_o), custom_call_target="tpu_custom_call" | custom-call | tf_op jit(solution)/shard_map/write_out/pallas_call | solution.py:279

commit v3 on v2

v3 whole, which is shorter than its diff:
```python
import functools

import jax
import jax.numpy as jnp
from jax import lax
from jax.experimental import pallas as pl
from jax.experimental.pallas import tpu as pltpu
from jax.sharding import PartitionSpec as P

PRIME = 65521
HALF = 32760
ONE = 2**21
MESH = pl.DeviceIdType.MESH
NX, NY, NZ = 4, 4, 8
FEATS = 128
ROWS = 16
K = 1024
H2 = 512
E = 128
HC = 512
F32 = jnp.float32
BF16 = jnp.bfloat16


def place():
    me = lax.axis_index("feat")
    return me, me // (NX * NY), (me // NX) % NY, me % NX


def wrap(value, size):
    return jnp.where(value >= size, value - size, value)


def fold(x):
    return (x >> 16) * 15 + (x & 65535)


def coefficient_rows(seeds):
    row = lax.broadcasted_iota(jnp.int32, (16, K), 0)
    shift = jnp.broadcast_to(seeds[1:2, :] + (PRIME - HALF), (16, K))
    x = fold(fold(jnp.where(row < 15, jnp.broadcast_to(seeds[0:1, :], (16, K)) << row, shift)))
    x = jnp.where(x >= PRIME, x - PRIME, x)
    x = jnp.where(x > HALF, x - PRIME, x)
    fixed = jnp.round(x.astype(F32) * F32(ONE / PRIME)).astype(jnp.int32)
    high = (fixed + 8192) >> 14
    rest = fixed - (high << 14)
    middle = (rest + 64) >> 7
    parts = [high << 14, middle << 7, rest - (middle << 7)]
    rows = [p.astype(F32) * F32(1.0 / ONE) for p in parts]
    return jnp.concatenate(rows + [jnp.zeros((128 - 48, K), F32)], axis=0)


def bits(ids, out, side):
    lane = lax.broadcasted_iota(jnp.int32, (1, 128), 1)
    row = lax.broadcasted_iota(jnp.int32, (16, 128), 0)
    turned = [ids] + [pltpu.roll(ids, ROWS * t, 1) for t in range(1, 8)]
    for y in range(NY):
        for x in range(NX):
            line = jnp.zeros((1, 128), jnp.int32)
            for z in range(NZ):
                r = 2 * z + y // 2
                piece = turned[(z - 4 * (y % 2) - x) % 8][r : r + 1, :]
                line = jnp.where(lane // ROWS == z, piece, line)
            wide = jnp.broadcast_to(line, (16, 128))
            bit = jnp.where(row < 15, (wide >> row) & 1, 1).astype(F32).astype(BF16)
            for r in range(0, 48, 16):
                out[NY * side + y, r : r + 16, x * 128 : (x + 1) * 128] = bit


def nt(left, right):
    return lax.dot_general(left, right, (((1,), (1,)), ((), ())), preferred_element_type=F32)


def kernel(
    g_hbm, ids_hbm, seeds_hbm, win_hbm, wout_hbm, acc, acc_o, enc, last,
    g_v, g_f, send, upper, ids_v, seeds_v, win_v, winT, wout_v, coef, bit, enc_a, enc_b, pre_a, pre_b, hid, slope,
    load, send_sem, recv_sem, ids_send, ids_recv, pass_send, pass_recv,
):
    me, mz, my, mx = place()
    core = lax.axis_index("dp")
    sibling = {"dp": 1 - core}
    loads = [
        pltpu.make_async_copy(g_hbm, g_v, load.at[0]),
        pltpu.make_async_copy(ids_hbm, ids_v.at[0], load.at[1]),
        pltpu.make_async_copy(seeds_hbm, seeds_v, load.at[2]),
        pltpu.make_async_copy(win_hbm.at[0, :, pl.ds(pl.multiple_of(core * H2, H2), H2)], win_v, load.at[3]),
        pltpu.make_async_copy(wout_hbm.at[0, pl.ds(pl.multiple_of(core * H2, H2), H2), :], wout_v, load.at[4]),
    ]
    for c in loads:
        c.start()

    barrier = pltpu.get_barrier_semaphore()

    @pl.loop(0, FEATS - 1, unroll=True)
    def _(i):
        other = jnp.where(i >= me, i + 1, i)
        pl.semaphore_signal(barrier, inc=1, device_id={"feat": other}, device_id_type=MESH)

    pl.semaphore_signal(barrier, inc=1, device_id=sibling, device_id_type=MESH)

    loads[0].wait()
    g_f[...] = g_v[...].astype(F32).reshape(ROWS * FEATS, E)

    @pl.loop(0, FEATS, unroll=8)
    def _(f):
        send[f] = g_f[pl.ds(f, ROWS, stride=FEATS), :].astype(BF16)

    slot = my * (NX * NZ) + mx * NZ + mz
    upper[0, slot] = send[me]
    loads[1].wait()

    ids_copy = pltpu.make_async_remote_copy(
        src_ref=ids_v.at[0], dst_ref=ids_v.at[1], send_sem=ids_send, recv_sem=ids_recv,
        device_id=sibling, device_id_type=MESH,
    )
    columns = [wrap(mz + dz, NZ) * (NX * NY) for dz in (0, 1, 7, 2, 6, 3, 5, 4)]

    def send_to(to, dy):
        pltpu.make_async_remote_copy(
            src_ref=send.at[to], dst_ref=upper.at[0, slot], send_sem=send_sem, recv_sem=recv_sem.at[dy],
            device_id={"feat": to}, device_id_type=MESH,
        ).start()

    def communicate():
        pl.semaphore_wait(barrier, FEATS)
        ids_copy.start()

        @pl.loop(0, NY)
        def _(dy):
            y = wrap(my + dy, NY) * NX

            @pl.loop(0, NX)
            def _(dx):
                near = y + wrap(mx + dx, NX)

                @pl.when(dy + dx > 0)
                def _():
                    send_to(columns[0] + near, dy)

                for column in columns[1:]:
                    send_to(column + near, dy)

    def home(q):
        return wrap(my - q + NY, NY)

    def encode(out, b):
        side = jnp.where(b >= NY, 1, 0)
        i = NY * side + home(b - NY * side)
        for r in range(0, K, 256):
            w = jnp.dot(coef[r : r + 256, :], bit[i], preferred_element_type=F32)
            code = ((w - jnp.round(w)) * F32(2.0 * PRIME / (PRIME - 1))).astype(BF16)
            out[r : r + 256, :] = code
            enc[b, r : r + 256, :] = code

    def forward(block, out):
        out[...] = jnp.dot(winT[...], block[...], preferred_element_type=F32)

    def activate(pre, b):
        for r in range(0, H2, 16):
            v = pre[r : r + 16, :]
            e = jnp.exp(jnp.minimum(v, 20.0))
            square = e * e
            half = 0.5 * square + e
            both = square + e
            inv = 1.0 / (half + 1.0)
            u = v * inv
            hid[b, r : r + 16, :] = (half * u).astype(BF16)
            slope[b, r : r + 16, :] = (half + both * u) * inv

    def prepare():
        loads[2].wait()
        coef[...] = jnp.transpose(coefficient_rows(seeds_v[...]))[:, :48].astype(BF16)
        loads[3].wait()
        for b in range(K // 128):
            winT[:, b * 128 : (b + 1) * 128] = jnp.transpose(win_v[b * 128 : (b + 1) * 128, :].astype(F32)).astype(BF16)
        bits(ids_v[0], bit, 0)
        encode(enc_a, 0)
        pre_b[...] = jnp.zeros_like(pre_b)

    def pair(j):
        @pl.when(j == 0)
        def _():
            prepare()

        @pl.when(j == 1)
        def _():
            ids_copy.wait()
            bits(ids_v[1], bit, 1)

        forward(enc_a, pre_a)
        encode(enc_b, 2 * j + 1)
        activate(pre_b, (2 * j + 7) % 8)
        forward(enc_b, pre_b)
        encode(enc_a, (2 * j + 2) % 8)
        activate(pre_a, 2 * j)

    turn = jnp.where(me < FEATS // 2, 1, 0)

    @pl.loop(0, NY + 1)
    def _(step):
        @pl.when(step == turn)
        def _():
            communicate()

        @pl.when(step != turn)
        def _():
            pair(jnp.where(step > turn, step - 1, step))

    activate(pre_b, 7)
    loads[4].wait()
    acc[...] = jnp.zeros_like(acc)
    acc_o[...] = jnp.zeros_like(acc_o)

    def received(q, count):
        first = home(q) * (NX * NZ)
        return pltpu.make_async_remote_copy(
            src_ref=send.at[pl.ds(0, count)], dst_ref=upper.at[0, pl.ds(first, count)], send_sem=send_sem,
            recv_sem=recv_sem.at[q], device_id=sibling, device_id_type=MESH,
        )

    def passed(q):
        first = home(q) * (NX * NZ)
        return pltpu.make_async_remote_copy(
            src_ref=upper.at[0, pl.ds(first, NX * NZ)], dst_ref=upper.at[1, pl.ds(first, NX * NZ)],
            send_sem=pass_send.at[q], recv_sem=pass_recv.at[q], device_id=sibling, device_id_type=MESH,
        )

    def arrive(q, count=NX * NZ):
        received(q, count).wait_recv()
        passed(q).start()

    def back(q, side):
        b = NY * side + q
        up = upper[side, pl.ds(home(q) * (NX * NZ), NX * NZ)].reshape(HC, E)
        back_pre = (nt(wout_v[...], up) * slope[b]).astype(BF16)
        acc_o[0] += jnp.dot(hid[b], up, preferred_element_type=F32)
        return back_pre

    def part(q, side):
        back_pre = back(q, side)
        acc[0] += nt(enc[NY * side + q], back_pre)

    arrive(0, NX * NZ - 1)

    @pl.loop(0, NY)
    def _(q):
        part(q, 0)

        @pl.when(q < NY - 2)
        def _():
            arrive(q + 1)

        @pl.when(q < NY - 1)
        def _():
            passed(q).wait()
            part(q, 1)

        @pl.when(q == NY - 2)
        def _():
            arrive(q + 1)

    passed(NY - 1).wait()
    last[...] = back(NY - 1, 1)
    pltpu.make_async_remote_copy(
        src_ref=send.at[pl.ds(0, FEATS - 1)], dst_ref=upper.at[0, pl.ds(0, FEATS - 1)], send_sem=send_sem,
        recv_sem=recv_sem.at[0], device_id=sibling, device_id_type=MESH,
    ).wait_send()


def finish(acc, acc_o, enc, last, gin_hbm, gout_hbm, total, sem):
    small = pltpu.make_async_copy(acc_o, gout_hbm, sem.at[0])
    small.start()
    copies = []
    for n, r in enumerate(range(0, K, 256)):
        total[r : r + 256, :] = acc[0, r : r + 256, :] + nt(enc[2 * NY - 1, r : r + 256, :], last[...])
        copy = pltpu.make_async_copy(total.at[pl.ds(r, 256)], gin_hbm.at[0, pl.ds(r, 256)], sem.at[n + 1])
        copy.start()
        copies.append(copy)
    for copy in copies:
        copy.wait()
    small.wait()


def on_device(grad_emb, ids, seeds, w_in, w_out):
    dma = pltpu.SemaphoreType.DMA
    sums = pl.pallas_call(
        kernel,
        out_shape=(
            pltpu.VMEM((1, K, H2), F32),
            pltpu.VMEM((1, H2, E), F32),
            pltpu.VMEM((2 * NY, K, HC), BF16),
            pltpu.VMEM((H2, HC), BF16),
        ),
        in_specs=[pl.BlockSpec(memory_space=pl.ANY)] * 5,
        out_specs=[pl.BlockSpec(memory_space=pltpu.VMEM)] * 4,
        scratch_shapes=[
            pltpu.VMEM((ROWS, FEATS, E), BF16),
            pltpu.VMEM((ROWS * FEATS, E), F32),
            pltpu.VMEM((FEATS, ROWS, E), BF16),
            pltpu.VMEM((2, FEATS, ROWS, E), BF16),
            pltpu.VMEM((2, 16, 128), jnp.int32),
            pltpu.VMEM((2, K), jnp.int32),
            pltpu.VMEM((K, H2), BF16),
            pltpu.VMEM((H2, K), BF16),
            pltpu.VMEM((H2, E), BF16),
            pltpu.VMEM((K, 48), BF16),
            pltpu.VMEM((2 * NY, 48, HC), BF16),
            pltpu.VMEM((K, HC), BF16),
            pltpu.VMEM((K, HC), BF16),
            pltpu.VMEM((H2, HC), F32),
            pltpu.VMEM((H2, HC), F32),
            pltpu.VMEM((2 * NY, H2, HC), BF16),
            pltpu.VMEM((2 * NY, H2, HC), F32),
            dma((5,)), dma, dma((NY,)), dma, dma, dma((NY,)), dma((NY,)),
        ],
        compiler_params=pltpu.CompilerParams(
            collective_id=0, has_side_effects=True, vmem_limit_bytes=40 * 2**20
        ),
        name="feature_backward",
    )(*[
        pltpu.with_memory_space_constraint(x, pltpu.HBM)
        for x in (grad_emb, ids.reshape(16, 128), seeds, w_in, w_out)
    ])
    return pl.pallas_call(
        finish,
        out_shape=(pltpu.HBM((1, K, H2), F32), pltpu.HBM((1, H2, E), F32)),
        in_specs=[pl.BlockSpec(memory_space=pltpu.VMEM)] * 4,
        out_specs=[pl.BlockSpec(memory_space=pltpu.HBM)] * 2,
        scratch_shapes=[pltpu.VMEM((K, H2), F32), dma((5,))],
        compiler_params=pltpu.CompilerParams(vmem_limit_bytes=8 * 2**20),
        name="finish",
    )(*[pltpu.with_memory_space_constraint(x, pltpu.VMEM) for x in sums])


def solution(mesh):
    return jax.shard_map(
        on_device,
        mesh=mesh,
        in_specs=(
            P(("dp", "feat"), None, None),
            P("dp", "feat"),
            P(),
            P("feat", None, None),
            P("feat", None, None),
        ),
        out_specs=(P("feat", None, "dp"), P("feat", "dp", None)),
        check_vma=False,
    )
```

time: 36.5 us -> 33.2 us (0.910)
  Pallas kernels: 35.7 us -> 32.5 us
    pallas_call x1, Pallas kernels: 34.3 us -> 30.8 us  [on_device(): pl.pallas_call(kernel, out_shape=(pltpu.VMEM((1, K, H2), F32), pltpu.VMEM...]
where the time goes in v3:
time: 33.2 us; the launch traced here: 33.1 us
  Pallas kernels  32.5 us (98%)
  between operations  0.64 us (2%)
    pallas_call x1, Pallas kernels, on_device(): pl.pallas_call(kernel, out_shape=(pltpu.VMEM((1, K, H2), F32), pltpu.VMEM...  30.8 us
    pallas_call x1, Pallas kernels, on_device(): pl.pallas_call(finish, out_shape=(pltpu.HBM((1, K, H2), F32), pltpu.HBM((...  1.69 us

profile of v3, /device:TPU:1, one launch (start us, length us, event | category | flops | bytes accessed | tf_op | source)
XLA Modules:
  0.0 33.1 jit_solution(5763244986265416435)
XLA Ops:
  0.6 30.8 %feature_backward.1 = (f32[1,1024,512]{2,1,0:T(8,128)S(1)}, f32[1,512,128]{2,1,0:T(8,128)S(1)}, bf16[8,1024,512]{2,1,0:T(8,128)(2,1)S(1)}, bf16[512,512]{1,0:T(8,128)(2,1)S(1)}) custom-call(bf16[16,128,128]{2,1,0:T(8,128)(2,1)} %g_hbm.1, s32[16,128]{1,0:T(8,128)} %bitcast.1, s32[2,1024]{1,0:T(2,128)} %seeds_hbm.1, bf16[1,1024,1024]{2,1,0:T(8,128)(2,1)} %win_hbm.1, ...), custom_call_target="tpu_custom_call" | custom-call | tf_op jit(solution)/shard_map/feature_backward/pallas_call | solution.py:286
  31.4 1.7 %finish.1 = (f32[1,1024,512]{2,1,0:T(8,128)}, f32[1,512,128]{2,1,0:T(8,128)}) custom-call(f32[1,1024,512]{2,1,0:T(8,128)S(1)} %get-tuple-element.6.acc, f32[1,512,128]{2,1,0:T(8,128)S(1)} %get-tuple-element.7.acc_o, bf16[8,1024,512]{2,1,0:T(8,128)(2,1)S(1)} %get-tuple-element.8.enc, bf16[512,512]{1,0:T(8,128)(2,1)S(1)} %get-tuple-element.9.last), custom_call_target="tpu_custom_call" | custom-call | tf_op jit(solution)/shard_map/finish/pallas_call | solution.py:324

commit v4 on v3

--- a/solution.py
+++ b/solution.py
@@ -29,6 +29,10 @@
 
 def wrap(value, size):
     return jnp.where(value >= size, value - size, value)
+
+
+def far_first(q):
+    return jnp.where(q == 0, 2, jnp.where(q == 1, 1, jnp.where(q == 2, 3, 0)))
 
 
 def fold(x):
@@ -91,7 +95,7 @@
 
     barrier = pltpu.get_barrier_semaphore()
 
-    @pl.loop(0, FEATS - 1, unroll=True)
+    @pl.loop(0, FEATS - 1)
     def _(i):
         other = jnp.where(i >= me, i + 1, i)
         pl.semaphore_signal(barrier, inc=1, device_id={"feat": other}, device_id_type=MESH)
@@ -113,11 +117,11 @@
         src_ref=ids_v.at[0], dst_ref=ids_v.at[1], send_sem=ids_send, recv_sem=ids_recv,
         device_id=sibling, device_id_type=MESH,
     )
-    columns = [wrap(mz + dz, NZ) * (NX * NY) for dz in (0, 1, 7, 2, 6, 3, 5, 4)]
-
-    def send_to(to, dy):
+    columns = [wrap(mz + dz, NZ) * (NX * NY) for dz in (4, 3, 5, 2, 6, 1, 7, 0)]
+
+    def send_to(to, q):
         pltpu.make_async_remote_copy(
-            src_ref=send.at[to], dst_ref=upper.at[0, slot], send_sem=send_sem, recv_sem=recv_sem.at[dy],
+            src_ref=send.at[to], dst_ref=upper.at[0, slot], send_sem=send_sem, recv_sem=recv_sem.at[q],
             device_id={"feat": to}, device_id_type=MESH,
         ).start()
 
@@ -126,22 +130,21 @@
         ids_copy.start()
 
         @pl.loop(0, NY)
-        def _(dy):
-            y = wrap(my + dy, NY) * NX
+        def _(q):
+            y = wrap(my + far_first(q), NY) * NX
 
             @pl.loop(0, NX)
-            def _(dx):
-                near = y + wrap(mx + dx, NX)
-
-                @pl.when(dy + dx > 0)
+            def _(p):
+                near = y + wrap(mx + far_first(p), NX)
+                for column in columns[:-1]:
+                    send_to(column + near, q)
+
+                @pl.when(q + p < NY + NX - 2)
                 def _():
-                    send_to(columns[0] + near, dy)
-
-                for column in columns[1:]:
-                    send_to(column + near, dy)
+                    send_to(columns[-1] + near, q)
 
     def home(q):
-        return wrap(my - q + NY, NY)
+        return wrap(my - far_first(q) + NY, NY)
 
     def encode(out, b):
         side = jnp.where(b >= NY, 1, 0)
@@ -225,7 +228,7 @@
             send_sem=pass_send.at[q], recv_sem=pass_recv.at[q], device_id=sibling, device_id_type=MESH,
         )
 
-    def arrive(q, count=NX * NZ):
+    def arrive(q, count):
         received(q, count).wait_recv()
         passed(q).start()
 
@@ -240,25 +243,24 @@
         back_pre = back(q, side)
         acc[0] += nt(enc[NY * side + q], back_pre)
 
-    arrive(0, NX * NZ - 1)
-
-    @pl.loop(0, NY)
+    arrive(0, NX * NZ)
+
+    @pl.loop(0, NY - 1)
     def _(q):
         part(q, 0)
 
         @pl.when(q < NY - 2)
         def _():
-            arrive(q + 1)
-
-        @pl.when(q < NY - 1)
-        def _():
-            passed(q).wait()
-            part(q, 1)
+            arrive(q + 1, NX * NZ)
 
         @pl.when(q == NY - 2)
         def _():
-            arrive(q + 1)
-
+            arrive(q + 1, NX * NZ - 1)
+
+        passed(q).wait()
+        part(q, 1)
+
+    part(NY - 1, 0)
     passed(NY - 1).wait()
     last[...] = back(NY - 1, 1)
     pltpu.make_async_remote_copy(

time: 33.2 us -> 32.6 us (0.982)
  Pallas kernels: 32.5 us -> 31.9 us
    pallas_call x1, Pallas kernels: 30.8 us -> 30.2 us  [on_device(): pl.pallas_call(kernel, out_shape=(pltpu.VMEM((1, K, H2), F32), pltpu.VMEM...]
where the time goes in v4:
time: 32.6 us; the launch traced here: 32.5 us
  Pallas kernels  31.9 us (98%)
  between operations  0.64 us (2%)
    pallas_call x1, Pallas kernels, on_device(): pl.pallas_call(kernel, out_shape=(pltpu.VMEM((1, K, H2), F32), pltpu.VMEM...  30.2 us
    pallas_call x1, Pallas kernels, on_device(): pl.pallas_call(finish, out_shape=(pltpu.HBM((1, K, H2), F32), pltpu.HBM((...  1.69 us

profile of v4, /device:TPU:1, one launch (start us, length us, event | category | flops | bytes accessed | tf_op | source)
XLA Modules:
  0.0 32.5 jit_solution(12831141851629940008)
XLA Ops:
  0.6 30.2 %feature_backward.1 = (f32[1,1024,512]{2,1,0:T(8,128)S(1)}, f32[1,512,128]{2,1,0:T(8,128)S(1)}, bf16[8,1024,512]{2,1,0:T(8,128)(2,1)S(1)}, bf16[512,512]{1,0:T(8,128)(2,1)S(1)}) custom-call(bf16[16,128,128]{2,1,0:T(8,128)(2,1)} %g_hbm.1, s32[16,128]{1,0:T(8,128)} %bitcast.1, s32[2,1024]{1,0:T(2,128)} %seeds_hbm.1, bf16[1,1024,1024]{2,1,0:T(8,128)(2,1)} %win_hbm.1, ...), custom_call_target="tpu_custom_call" | custom-call | tf_op jit(solution)/shard_map/feature_backward/pallas_call | solution.py:288
  30.8 1.7 %finish.1 = (f32[1,1024,512]{2,1,0:T(8,128)}, f32[1,512,128]{2,1,0:T(8,128)}) custom-call(f32[1,1024,512]{2,1,0:T(8,128)S(1)} %get-tuple-element.6.acc, f32[1,512,128]{2,1,0:T(8,128)S(1)} %get-tuple-element.7.acc_o, bf16[8,1024,512]{2,1,0:T(8,128)(2,1)S(1)} %get-tuple-element.8.enc, bf16[512,512]{1,0:T(8,128)(2,1)S(1)} %get-tuple-element.9.last), custom_call_target="tpu_custom_call" | custom-call | tf_op jit(solution)/shard_map/finish/pallas_call | solution.py:326

commit v5 on v4

--- a/solution.py
+++ b/solution.py
@@ -95,7 +95,7 @@
 
     barrier = pltpu.get_barrier_semaphore()
 
-    @pl.loop(0, FEATS - 1)
+    @pl.loop(0, FEATS - 1, unroll=True)
     def _(i):
         other = jnp.where(i >= me, i + 1, i)
         pl.semaphore_signal(barrier, inc=1, device_id={"feat": other}, device_id_type=MESH)
@@ -170,6 +170,8 @@
             hid[b, r : r + 16, :] = (half * u).astype(BF16)
             slope[b, r : r + 16, :] = (half + both * u) * inv
 
+    turn = jnp.where(me < FEATS // 4, 2, jnp.where(me < FEATS // 2, 1, 0))
+
     def prepare():
         loads[2].wait()
         coef[...] = jnp.transpose(coefficient_rows(seeds_v[...]))[:, :48].astype(BF16)
@@ -185,10 +187,14 @@
         def _():
             prepare()
 
-        @pl.when(j == 1)
-        def _():
-            ids_copy.wait()
+        @pl.when(j == jnp.maximum(turn, 1))
+        def _():
+            ids_copy.wait_recv()
             bits(ids_v[1], bit, 1)
+
+            @pl.when(j == 2)
+            def _():
+                encode(enc_a, NY)
 
         forward(enc_a, pre_a)
         encode(enc_b, 2 * j + 1)
@@ -197,8 +203,6 @@
         encode(enc_a, (2 * j + 2) % 8)
         activate(pre_a, 2 * j)
 
-    turn = jnp.where(me < FEATS // 2, 1, 0)
-
     @pl.loop(0, NY + 1)
     def _(step):
         @pl.when(step == turn)
@@ -257,16 +261,19 @@
         def _():
             arrive(q + 1, NX * NZ - 1)
 
-        passed(q).wait()
+        passed(q).wait_recv()
         part(q, 1)
 
     part(NY - 1, 0)
-    passed(NY - 1).wait()
+    passed(NY - 1).wait_recv()
     last[...] = back(NY - 1, 1)
     pltpu.make_async_remote_copy(
         src_ref=send.at[pl.ds(0, FEATS - 1)], dst_ref=upper.at[0, pl.ds(0, FEATS - 1)], send_sem=send_sem,
         recv_sem=recv_sem.at[0], device_id=sibling, device_id_type=MESH,
     ).wait_send()
+    ids_copy.wait_send()
+    for q in range(NY):
+        passed(q).wait_send()
 
 
 def finish(acc, acc_o, enc, last, gin_hbm, gout_hbm, total, sem):

time: 32.6 us -> 31.6 us (0.969)
  Pallas kernels: 31.9 us -> 30.9 us
    pallas_call x1, Pallas kernels: 30.2 us -> 29.2 us  [on_device(): pl.pallas_call(kernel, out_shape=(pltpu.VMEM((1, K, H2), F32), pltpu.VMEM...]
where the time goes in v5:
time: 31.6 us; the launch traced here: 31.5 us
  Pallas kernels  30.9 us (98%)
  between operations  0.64 us (2%)
    pallas_call x1, Pallas kernels, on_device(): pl.pallas_call(kernel, out_shape=(pltpu.VMEM((1, K, H2), F32), pltpu.VMEM...  29.2 us
    pallas_call x1, Pallas kernels, on_device(): pl.pallas_call(finish, out_shape=(pltpu.HBM((1, K, H2), F32), pltpu.HBM((...  1.69 us

profile of v5, /device:TPU:1, one launch (start us, length us, event | category | flops | bytes accessed | tf_op | source)
XLA Modules:
  0.0 31.5 jit_solution(7322602775770139915)
XLA Ops:
  0.6 29.2 %feature_backward.1 = (f32[1,1024,512]{2,1,0:T(8,128)S(1)}, f32[1,512,128]{2,1,0:T(8,128)S(1)}, bf16[8,1024,512]{2,1,0:T(8,128)(2,1)S(1)}, bf16[512,512]{1,0:T(8,128)(2,1)S(1)}) custom-call(bf16[16,128,128]{2,1,0:T(8,128)(2,1)} %g_hbm.1, s32[16,128]{1,0:T(8,128)} %bitcast.1, s32[2,1024]{1,0:T(2,128)} %seeds_hbm.1, bf16[1,1024,1024]{2,1,0:T(8,128)(2,1)} %win_hbm.1, ...), custom_call_target="tpu_custom_call" | custom-call | tf_op jit(solution)/shard_map/feature_backward/pallas_call | solution.py:295
  29.8 1.7 %finish.1 = (f32[1,1024,512]{2,1,0:T(8,128)}, f32[1,512,128]{2,1,0:T(8,128)}) custom-call(f32[1,1024,512]{2,1,0:T(8,128)S(1)} %get-tuple-element.6.acc, f32[1,512,128]{2,1,0:T(8,128)S(1)} %get-tuple-element.7.acc_o, bf16[8,1024,512]{2,1,0:T(8,128)(2,1)S(1)} %get-tuple-element.8.enc, bf16[512,512]{1,0:T(8,128)(2,1)S(1)} %get-tuple-element.9.last), custom_call_target="tpu_custom_call" | custom-call | tf_op jit(solution)/shard_map/finish/pallas_call | solution.py:333

commit v6 on v5

--- a/solution.py
+++ b/solution.py
@@ -18,6 +18,7 @@
 H2 = 512
 E = 128
 HC = 512
+FAR = (2, 1, 3, 0)
 F32 = jnp.float32
 BF16 = jnp.bfloat16
 
@@ -94,12 +95,17 @@
         c.start()
 
     barrier = pltpu.get_barrier_semaphore()
-
-    @pl.loop(0, FEATS - 1, unroll=True)
-    def _(i):
-        other = jnp.where(i >= me, i + 1, i)
+    columns = [wrap(mz + dz, NZ) * (NX * NY) for dz in (4, 3, 5, 2, 6, 1, 7, 0)]
+
+    def greet(other):
         pl.semaphore_signal(barrier, inc=1, device_id={"feat": other}, device_id_type=MESH)
 
+    for q in FAR:
+        y = wrap(my + q, NY) * NX
+        for p in FAR:
+            near = y + wrap(mx + p, NX)
+            for column in columns[:-1] if p + q == 0 else columns:
+                greet(column + near)
     pl.semaphore_signal(barrier, inc=1, device_id=sibling, device_id_type=MESH)
 
     loads[0].wait()
@@ -117,8 +123,6 @@
         src_ref=ids_v.at[0], dst_ref=ids_v.at[1], send_sem=ids_send, recv_sem=ids_recv,
         device_id=sibling, device_id_type=MESH,
     )
-    columns = [wrap(mz + dz, NZ) * (NX * NY) for dz in (4, 3, 5, 2, 6, 1, 7, 0)]
-
     def send_to(to, q):
         pltpu.make_async_remote_copy(
             src_ref=send.at[to], dst_ref=upper.at[0, slot], send_sem=send_sem, recv_sem=recv_sem.at[q],
@@ -170,7 +174,7 @@
             hid[b, r : r + 16, :] = (half * u).astype(BF16)
             slope[b, r : r + 16, :] = (half + both * u) * inv
 
-    turn = jnp.where(me < FEATS // 4, 2, jnp.where(me < FEATS // 2, 1, 0))
+    turn = jnp.where(me < FEATS * 3 // 16, 2, jnp.where(me < FEATS // 2, 1, 0))
 
     def prepare():
         loads[2].wait()

time: 31.6 us -> 31.2 us (0.987)
  Pallas kernels: 30.9 us -> 30.5 us
    pallas_call x1, Pallas kernels: 29.2 us -> 28.8 us  [on_device(): pl.pallas_call(kernel, out_shape=(pltpu.VMEM((1, K, H2), F32), pltpu.VMEM...]
where the time goes in v6:
time: 31.2 us; the launch traced here: 31.1 us
  Pallas kernels  30.5 us (98%)
  between operations  0.64 us (2%)
    pallas_call x1, Pallas kernels, on_device(): pl.pallas_call(kernel, out_shape=(pltpu.VMEM((1, K, H2), F32), pltpu.VMEM...  28.8 us
    pallas_call x1, Pallas kernels, on_device(): pl.pallas_call(finish, out_shape=(pltpu.HBM((1, K, H2), F32), pltpu.HBM((...  1.69 us

profile of v6, /device:TPU:1, one launch (start us, length us, event | category | flops | bytes accessed | tf_op | source)
XLA Modules:
  0.0 31.1 jit_solution(3929781994129073466)
XLA Ops:
  0.6 28.8 %feature_backward.1 = (f32[1,1024,512]{2,1,0:T(8,128)S(1)}, f32[1,512,128]{2,1,0:T(8,128)S(1)}, bf16[8,1024,512]{2,1,0:T(8,128)(2,1)S(1)}, bf16[512,512]{1,0:T(8,128)(2,1)S(1)}) custom-call(bf16[16,128,128]{2,1,0:T(8,128)(2,1)} %g_hbm.1, s32[16,128]{1,0:T(8,128)} %bitcast.1, s32[2,1024]{1,0:T(2,128)} %seeds_hbm.1, bf16[1,1024,1024]{2,1,0:T(8,128)(2,1)} %win_hbm.1, ...), custom_call_target="tpu_custom_call" | custom-call | tf_op jit(solution)/shard_map/feature_backward/pallas_call | solution.py:299
  29.4 1.7 %finish.1 = (f32[1,1024,512]{2,1,0:T(8,128)}, f32[1,512,128]{2,1,0:T(8,128)}) custom-call(f32[1,1024,512]{2,1,0:T(8,128)S(1)} %get-tuple-element.6.acc, f32[1,512,128]{2,1,0:T(8,128)S(1)} %get-tuple-element.7.acc_o, bf16[8,1024,512]{2,1,0:T(8,128)(2,1)S(1)} %get-tuple-element.8.enc, bf16[512,512]{1,0:T(8,128)(2,1)S(1)} %get-tuple-element.9.last), custom_call_target="tpu_custom_call" | custom-call | tf_op jit(solution)/shard_map/finish/pallas_call | solution.py:337
